TPU v7x, 512 devices: a whole 4x4x16 slice. The times are simulated.
512 devices in a mesh: gx: 128 (over x, y_hi, z), gy: 2 (over core), gz: 2 (over y_lo).
Axes of the slice: x: 4, y: 4 (y_hi: 2, y_lo: 2; y = y_hi * 2 + y_lo), z: 16, core: 2. Of those that a mesh axis runs over, the one named last changes fastest.
Arguments:
- concentration_levels: float32 [3, 17, 512, 16, 256], P(None, None, 'gx', 'gz', 'gy'), may hold values from 0.0001 to 1
- thermal_levels: float32 [3, 512, 16, 256], P(None, 'gx', 'gz', 'gy'), may hold values from 4 to 6
- fluid_velocity: float32 [3, 512, 16, 256], P(None, 'gx', 'gz', 'gy'), may hold values from -4 to 4
- diffusivity: float32 [18], replicated, may hold values from 0.15 to 0.6
- natural_logged_prefactors: float32 [73], replicated, may hold values from -3 to 0
- energy_barrier_kelvin: float32 [73], replicated, may hold values from 1 to 8
- enthalpy_yield_per_mole: float32 [17], replicated, may hold values from -0.3 to 0.3
- stoichiometric_member_table: int32 [4, 73], replicated, may hold values from 0 to 17
Outputs:
- species_next: float32 [17, 512, 16, 256], P(None, 'gx', 'gz', 'gy')
- temperature_next: float32 [512, 16, 256], P('gx', 'gz', 'gy')
Inputs may be any that keep to these rules, and one draw needn't show every extreme that they name: `stoichiometric_member_table`: rows 0 and 1 give each reaction's two reactants and rows 2 and 3 its two products; the value 17 means the collision partner M in rows 0 and 1 and no product in rows 2 and 3.
All inputs are finite; a program needn't handle non-finite values.
Results may differ from a plain program's by a relative error of at most 0.0003.
Values sent between devices are 32-bit elements; how exact they have to be, the bound alone decides.
A program may use at most 64 MiB of HBM per device.

v0:
```python
import jax
import jax.numpy as jnp
from jax import lax
from jax.sharding import PartitionSpec as P

time_step = 0.125
first_coeffs = (4.0 / 5.0, -1.0 / 5.0, 4.0 / 105.0, -1.0 / 280.0)
second_coeffs = (8.0 / 5.0, -1.0 / 5.0, 8.0 / 315.0, -1.0 / 560.0)
center_coeff = -205.0 / 72.0


def with_halo(block, sides, width):
    for axis, dim in sides:
        count = lax.axis_size(axis)
        forward = [(i, i + 1) for i in range(count - 1)]
        forward.append((count - 1, 0))
        backward = [(target, source) for source, target in forward]
        low = lax.ppermute(
            lax.slice_in_dim(block, block.shape[dim] - width, None, axis=dim), axis, forward
        )
        high = lax.ppermute(lax.slice_in_dim(block, 0, width, axis=dim), axis, backward)
        block = jnp.concatenate([low, block, high], axis=dim)
    return block


def stencils(padded, direction, length_cells):

    def shifted(offset):
        return lax.slice_in_dim(padded, 4 + offset, 4 + offset + length_cells, axis=direction)

    gradient = first_coeffs[0] * (shifted(1) - shifted(-1))
    curvature = center_coeff * shifted(0) + second_coeffs[0] * (shifted(1) + shifted(-1))
    for offset in range(1, 4):
        gradient = gradient + first_coeffs[offset] * (shifted(offset + 1) - shifted(-offset - 1))
        curvature = curvature + second_coeffs[offset] * (shifted(offset + 1) + shifted(-offset - 1))
    return (gradient, curvature)


def combustion_source_terms(
    mixture_constituent,
    mixture_warmth_kelvin,
    natural_logged_prefactors,
    energy_barrier_kelvin,
    enthalpy_yield_per_mole,
    stoichiometric_member_table,
):
    count_species = mixture_constituent.shape[0]
    expanded_array_extent = (slice(None),) + (None,) * mixture_warmth_kelvin.ndim
    forward_speed_constants = jnp.exp(
        natural_logged_prefactors[expanded_array_extent]
        - energy_barrier_kelvin[expanded_array_extent] / mixture_warmth_kelvin[None]
    )
    partner = jnp.mean(mixture_constituent, axis=0)
    lookup = jnp.concatenate([mixture_constituent, partner[None]], axis=0)
    progress = (
        forward_speed_constants
        * jnp.take(lookup, stoichiometric_member_table[0], axis=0)
        * jnp.take(lookup, stoichiometric_member_table[1], axis=0)
    )
    labels = jnp.arange(count_species + 1, dtype=jnp.int32)[:, None]

    def onehot(which_row):
        return (labels == stoichiometric_member_table[which_row][None, :]).astype(jnp.float32)

    stoich = (onehot(2) + onehot(3) - onehot(0) - onehot(1))[:count_species]
    production = jnp.tensordot(stoich, progress, axes=1, precision=lax.Precision.HIGHEST)
    release = jnp.tensordot(
        enthalpy_yield_per_mole, production, axes=1, precision=lax.Precision.HIGHEST
    )
    return (production, release)


def tendency(
    extended,
    padded_z,
    padded_y,
    interior,
    velocity,
    diffusivity,
    natural_logged_prefactors,
    energy_barrier_kelvin,
    enthalpy_yield_per_mole,
    stoichiometric_member_table,
):
    count_species = interior.shape[0] - 1
    grad_x, curv_x = stencils(extended, 1, interior.shape[1])
    grad_z, curv_z = stencils(padded_z, 2, interior.shape[2])
    grad_y, curv_y = stencils(padded_y, 3, interior.shape[3])
    transport = velocity[0][None] * grad_x + velocity[1][None] * grad_y + velocity[2][None] * grad_z
    laplace = curv_x + curv_y + curv_z
    diffusion = diffusivity[:, None, None, None]
    change = diffusion * laplace - transport
    production, release = combustion_source_terms(
        interior[:count_species],
        interior[count_species],
        natural_logged_prefactors,
        energy_barrier_kelvin,
        enthalpy_yield_per_mole,
        stoichiometric_member_table,
    )
    return jnp.concatenate(
        [change[:count_species] + production, (change[count_species] + release)[None]], axis=0
    )


def evaluate(state, borders, velocity, constants):
    cells_z = state.shape[2]
    cells_y = state.shape[3]
    extended = jnp.concatenate([borders[0], state, borders[1]], axis=1)
    padded = with_halo(state, (("gy", 3), ("gz", 2)), 4)
    padded_z = padded[:, :, :, 4 : 4 + cells_y]
    padded_y = padded[:, :, 4 : 4 + cells_z, :]
    return tendency(extended, padded_z, padded_y, state, velocity, *constants)


def advance(current, newer, older, velocity, constants):
    delayed_first = (2.0 * newer[0] - older[0], 2.0 * newer[1] - older[1])
    first_rate = evaluate(current, delayed_first, velocity, constants)
    predictor = current + time_step * first_rate
    delayed_second = (3.0 * newer[0] - 2.0 * older[0], 3.0 * newer[1] - 2.0 * older[1])
    second_rate = evaluate(predictor, delayed_second, velocity, constants)
    return current + 0.5 * time_step * (first_rate + second_rate)


def local(
    concentration_levels,
    thermal_levels,
    fluid_velocity,
    diffusivity,
    natural_logged_prefactors,
    energy_barrier_kelvin,
    enthalpy_yield_per_mole,
    stoichiometric_member_table,
):
    count_species = concentration_levels.shape[1]
    cells_x = concentration_levels.shape[2]
    time_levels = [
        jnp.concatenate(
            [concentration_levels[level_index], thermal_levels[level_index][None]], axis=0
        )
        for level_index in range(3)
    ]
    gathered = with_halo(jnp.stack(time_levels), (("gx", 2),), 4)
    borders = [
        (gathered[level_index, :, :4], gathered[level_index, :, cells_x + 4 :])
        for level_index in range(3)
    ]
    constants = (
        diffusivity,
        natural_logged_prefactors,
        energy_barrier_kelvin,
        enthalpy_yield_per_mole,
        stoichiometric_member_table,
    )
    stepped = advance(time_levels[2], borders[1], borders[0], fluid_velocity, constants)
    final_state = advance(stepped, borders[2], borders[1], fluid_velocity, constants)
    return (final_state[:count_species], final_state[count_species])


def solution(mesh):
    in_specs = (
        P(None, None, "gx", "gz", "gy"),
        P(None, "gx", "gz", "gy"),
        P(None, "gx", "gz", "gy"),
        P(),
        P(),
        P(),
        P(),
        P(),
    )
    out_specs = (P(None, "gx", "gz", "gy"), P("gx", "gz", "gy"))
    return jax.shard_map(local, mesh=mesh, in_specs=in_specs, out_specs=out_specs, check_vma=False)
```

profile of v0, /device:TPU:16, one launch (start us, length us, event | category | flops | bytes accessed | tf_op | source)
XLA Modules:
  0.0 156.9 jit_solution(10748146056047574174)
XLA Ops:
  3.7 11.2 %collective-permute-start = (f32[3,18,4,8,128]{4,3,2,1,0:T(8,128)}, f32[3,18,4,8,128]{4,3,2,1,0:T(8,128)}, u32[]{:S(2)}, u32[]{:S(2)}) collective-permute-start(f32[3,18,4,8,128]{4,3,2,1,0:T(8,128)} %pad_maximum_fusion.4), channel_id=1, source_target_pairs={{4,0},{8,4},{12,8},{16,12},{20,16},{24,20},{28,24},{32,28},{36,32}... | collective-permute-start | bytes 2654216 | tf_op jit(solution)/shard_map/ppermute | solution.py:21
  14.9 1.9 %collective-permute-start.1 = (f32[3,18,4,8,128]{4,3,2,1,0:T(8,128)}, f32[3,18,4,8,128]{4,3,2,1,0:T(8,128)}, u32[]{:S(2)}, u32[]{:S(2)}) collective-permute-start(f32[3,18,4,8,128]{4,3,2,1,0:T(8,128)} %pad_maximum_fusion.4), channel_id=1, source_target_pairs={{0,4},{4,8},{8,12},{12,16},{16,20},{20,24},{24,28},{28,32},{32,36}... | collective-permute-start | bytes 2654216 | tf_op jit(solution)/shard_map/ppermute | solution.py:18
  19.7 2.4 %collective-permute-start.3 = (f32[18,4,8,4]{3,2,1,0:T(8,128)}, f32[18,4,8,4]{3,2,1,0:T(8,128)}, u32[]{:S(2)}, u32[]{:S(2)}) collective-permute-start(f32[18,4,8,4]{3,2,1,0:T(8,128)} %get-tuple-element.55), channel_id=1, source_target_pairs={{0,2},{2,0},{1,3},{3,1},{4,6},{6,4},{5,7},{7,5},{8,10},{10,8},{9,1... | collective-permute-start | bytes 27656 | tf_op jit(solution)/shard_map/ppermute | solution.py:18
  27.2 4.1 %collective-permute-start.4 = (f32[18,4,4,136]{3,2,1,0:T(4,128)S(1)}, f32[18,4,4,136]{3,2,1,0:T(4,128)S(1)}, u32[]{:S(2)}, u32[]{:S(2)}) collective-permute-start(f32[18,4,4,136]{3,2,1,0:T(4,128)S(1)} %get-tuple-element.37), channel_id=1, source_target_pairs={{1,0},{0,1},{3,2},{2,3},{5,4},{4,5},{7,6},{6,7},{9,8},{8,9},{11,10... | collective-permute-start | bytes 470024 | tf_op jit(solution)/shard_map/ppermute | solution.py:21
  34.5 18.9 %collective-permute-done.4 = f32[18,4,4,136]{3,2,1,0:T(4,128)S(1)} collective-permute-done((f32[18,4,4,136]{3,2,1,0:T(4,128)S(1)}, f32[18,4,4,136]{3,2,1,0:T(4,128)S(1)}, u32[]{:S(2)}, u32[]{:S(2)}) %collective-permute-start.4) | collective-permute-done | bytes 156704 | tf_op jit(solution)/shard_map/ppermute | solution.py:21
  53.4 6.3 %collective-permute-done.5 = f32[18,4,4,136]{3,2,1,0:T(4,128)S(1)} collective-permute-done((f32[18,4,4,136]{3,2,1,0:T(4,128)S(1)}, f32[18,4,4,136]{3,2,1,0:T(4,128)S(1)}, u32[]{:S(2)}, u32[]{:S(2)}) %collective-permute-start.5) | collective-permute-done | bytes 156704 | tf_op jit(solution)/shard_map/ppermute | solution.py:18
  61.5 2.1 %subtract_bitcast_fusion.1 = (f32[18,4,8,128]{3,2,1,0:T(8,128)}, f32[18,4,8,128]{3,2,1,0:T(8,128)}, f32[18,4,8,128]{3,2,1,0:T(8,128)S(1)}, f32[18,4,8,128]{3,2,1,0:T(8,128)}) fusion(f32[3,18,4,8,128]{4,3,2,1,0:T(8,128)} %collective-permute-done), kind=kLoop, calls=%fused_computation.176 | loop fusion | flops 663552 | bytes 2064384 | tf_op jit(solution)/shard_map/sub | solution.py:120
  63.6 2.1 %subtract_bitcast_fusion = (f32[18,4,8,128]{3,2,1,0:T(8,128)}, f32[18,4,8,128]{3,2,1,0:T(8,128)}, f32[18,4,8,128]{3,2,1,0:T(8,128)S(1)}, f32[18,4,8,128]{3,2,1,0:T(8,128)}) fusion(f32[3,18,4,8,128]{4,3,2,1,0:T(8,128)} %collective-permute-done.1), kind=kLoop, calls=%fused_computation.175 | loop fusion | flops 663552 | bytes 2064384 | tf_op jit(solution)/shard_map/sub | solution.py:120
  71.0 2.0 %collective-permute-start.6 = (f32[18,4,8,4]{3,2,1,0:T(8,128)S(1)}, f32[18,4,8,4]{3,2,1,0:T(8,128)S(1)}, u32[]{:S(2)}, u32[]{:S(2)}) collective-permute-start(f32[18,4,8,4]{3,2,1,0:T(8,128)S(1)} %get-tuple-element.48), channel_id=1, source_target_pairs={{2,0},{0,2},{3,1},{1,3},{6,4},{4,6},{7,5},{5,7},{10,8},{8,10},{11,... | collective-permute-start | bytes 27656 | tf_op jit(solution)/shard_map/ppermute | solution.py:21
  73.0 2.4 %collective-permute-start.7 = (f32[18,4,8,4]{3,2,1,0:T(8,128)S(1)}, f32[18,4,8,4]{3,2,1,0:T(8,128)S(1)}, u32[]{:S(2)}, u32[]{:S(2)}) collective-permute-start(f32[18,4,8,4]{3,2,1,0:T(8,128)S(1)} %get-tuple-element.47), channel_id=1, source_target_pairs={{0,2},{2,0},{1,3},{3,1},{4,6},{6,4},{5,7},{7,5},{8,10},{10,8},{9,1... | collective-permute-start | bytes 27656 | tf_op jit(solution)/shard_map/ppermute | solution.py:18
  77.7 2.7 %collective-permute-start.8 = (f32[18,4,4,136]{3,2,1,0:T(4,128)S(1)}, f32[18,4,4,136]{3,2,1,0:T(4,128)S(1)}, u32[]{:S(2)}, u32[]{:S(2)}) collective-permute-start(f32[18,4,4,136]{3,2,1,0:T(4,128)S(1)} %get-tuple-element.35), channel_id=1, source_target_pairs={{1,0},{0,1},{3,2},{2,3},{5,4},{4,5},{7,6},{6,7},{9,8},{8,9},{11,10... | collective-permute-start | bytes 470024 | tf_op jit(solution)/shard_map/ppermute | solution.py:21
  80.4 3.4 %collective-permute-start.9 = (f32[18,4,4,136]{3,2,1,0:T(4,128)S(1)}, f32[18,4,4,136]{3,2,1,0:T(4,128)S(1)}, u32[]{:S(2)}, u32[]{:S(2)}) collective-permute-start(f32[18,4,4,136]{3,2,1,0:T(4,128)S(1)} %get-tuple-element.36), channel_id=1, source_target_pairs={{0,1},{1,0},{2,3},{3,2},{4,5},{5,4},{6,7},{7,6},{8,9},{9,8},{10,11... | collective-permute-start | bytes 470024 | tf_op jit(solution)/shard_map/ppermute | solution.py:18
  84.2 5.3 %collective-permute-done.8 = f32[18,4,4,136]{3,2,1,0:T(4,128)S(1)} collective-permute-done((f32[18,4,4,136]{3,2,1,0:T(4,128)S(1)}, f32[18,4,4,136]{3,2,1,0:T(4,128)S(1)}, u32[]{:S(2)}, u32[]{:S(2)}) %collective-permute-start.8) | collective-permute-done | bytes 156704 | tf_op jit(solution)/shard_map/ppermute | solution.py:21
  89.5 5.4 %collective-permute-done.9 = f32[18,4,4,136]{3,2,1,0:T(4,128)S(1)} collective-permute-done((f32[18,4,4,136]{3,2,1,0:T(4,128)S(1)}, f32[18,4,4,136]{3,2,1,0:T(4,128)S(1)}, u32[]{:S(2)}, u32[]{:S(2)}) %collective-permute-start.9) | collective-permute-done | bytes 156704 | tf_op jit(solution)/shard_map/ppermute | solution.py:18
  101.6 2.4 %collective-permute-start.11 = (f32[18,4,8,4]{3,2,1,0:T(8,128)S(1)}, f32[18,4,8,4]{3,2,1,0:T(8,128)S(1)}, u32[]{:S(2)}, u32[]{:S(2)}) collective-permute-start(f32[18,4,8,4]{3,2,1,0:T(8,128)S(1)} %get-tuple-element.43), channel_id=1, source_target_pairs={{0,2},{2,0},{1,3},{3,1},{4,6},{6,4},{5,7},{7,5},{8,10},{10,8},{9,1... | collective-permute-start | bytes 27656 | tf_op jit(solution)/shard_map/ppermute | solution.py:18
  106.3 2.6 %collective-permute-start.12 = (f32[18,4,4,136]{3,2,1,0:T(4,128)S(1)}, f32[18,4,4,136]{3,2,1,0:T(4,128)S(1)}, u32[]{:S(2)}, u32[]{:S(2)}) collective-permute-start(f32[18,4,4,136]{3,2,1,0:T(4,128)S(1)} %get-tuple-element.33), channel_id=1, source_target_pairs={{1,0},{0,1},{3,2},{2,3},{5,4},{4,5},{7,6},{6,7},{9,8},{8,9},{11,10... | collective-permute-start | bytes 470024 | tf_op jit(solution)/shard_map/ppermute | solution.py:21
  109.0 3.2 %collective-permute-start.13 = (f32[18,4,4,136]{3,2,1,0:T(4,128)S(1)}, f32[18,4,4,136]{3,2,1,0:T(4,128)S(1)}, u32[]{:S(2)}, u32[]{:S(2)}) collective-permute-start(f32[18,4,4,136]{3,2,1,0:T(4,128)S(1)} %get-tuple-element.34), channel_id=1, source_target_pairs={{0,1},{1,0},{2,3},{3,2},{4,5},{5,4},{6,7},{7,6},{8,9},{9,8},{10,11... | collective-permute-start | bytes 470024 | tf_op jit(solution)/shard_map/ppermute | solution.py:18
  112.5 5.5 %collective-permute-done.12 = f32[18,4,4,136]{3,2,1,0:T(4,128)S(1)} collective-permute-done((f32[18,4,4,136]{3,2,1,0:T(4,128)S(1)}, f32[18,4,4,136]{3,2,1,0:T(4,128)S(1)}, u32[]{:S(2)}, u32[]{:S(2)}) %collective-permute-start.12) | collective-permute-done | bytes 156704 | tf_op jit(solution)/shard_map/ppermute | solution.py:21
  118.1 5.4 %collective-permute-done.13 = f32[18,4,4,136]{3,2,1,0:T(4,128)S(1)} collective-permute-done((f32[18,4,4,136]{3,2,1,0:T(4,128)S(1)}, f32[18,4,4,136]{3,2,1,0:T(4,128)S(1)}, u32[]{:S(2)}, u32[]{:S(2)}) %collective-permute-start.13) | collective-permute-done | bytes 156704 | tf_op jit(solution)/shard_map/ppermute | solution.py:18
  130.6 2.6 %collective-permute-start.15 = (f32[18,4,8,4]{3,2,1,0:T(8,128)S(1)}, f32[18,4,8,4]{3,2,1,0:T(8,128)S(1)}, u32[]{:S(2)}, u32[]{:S(2)}) collective-permute-start(f32[18,4,8,4]{3,2,1,0:T(8,128)S(1)} %get-tuple-element.39), channel_id=1, source_target_pairs={{0,2},{2,0},{1,3},{3,1},{4,6},{6,4},{5,7},{7,5},{8,10},{10,8},{9,1... | collective-permute-start | bytes 27656 | tf_op jit(solution)/shard_map/ppermute | solution.py:18
  135.5 2.6 %collective-permute-start.16 = (f32[18,4,4,136]{3,2,1,0:T(4,128)S(1)}, f32[18,4,4,136]{3,2,1,0:T(4,128)S(1)}, u32[]{:S(2)}, u32[]{:S(2)}) collective-permute-start(f32[18,4,4,136]{3,2,1,0:T(4,128)S(1)} %get-tuple-element.31), channel_id=1, source_target_pairs={{1,0},{0,1},{3,2},{2,3},{5,4},{4,5},{7,6},{6,7},{9,8},{8,9},{11,10... | collective-permute-start | bytes 470024 | tf_op jit(solution)/shard_map/ppermute | solution.py:21
  138.1 3.2 %collective-permute-start.17 = (f32[18,4,4,136]{3,2,1,0:T(4,128)S(1)}, f32[18,4,4,136]{3,2,1,0:T(4,128)S(1)}, u32[]{:S(2)}, u32[]{:S(2)}) collective-permute-start(f32[18,4,4,136]{3,2,1,0:T(4,128)S(1)} %get-tuple-element.32), channel_id=1, source_target_pairs={{0,1},{1,0},{2,3},{3,2},{4,5},{5,4},{6,7},{7,6},{8,9},{9,8},{10,11... | collective-permute-start | bytes 470024 | tf_op jit(solution)/shard_map/ppermute | solution.py:18
  141.8 5.5 %collective-permute-done.16 = f32[18,4,4,136]{3,2,1,0:T(4,128)S(1)} collective-permute-done((f32[18,4,4,136]{3,2,1,0:T(4,128)S(1)}, f32[18,4,4,136]{3,2,1,0:T(4,128)S(1)}, u32[]{:S(2)}, u32[]{:S(2)}) %collective-permute-start.16) | collective-permute-done | bytes 156704 | tf_op jit(solution)/shard_map/ppermute | solution.py:21
  147.3 5.4 %collective-permute-done.17 = f32[18,4,4,136]{3,2,1,0:T(4,128)S(1)} collective-permute-done((f32[18,4,4,136]{3,2,1,0:T(4,128)S(1)}, f32[18,4,4,136]{3,2,1,0:T(4,128)S(1)}, u32[]{:S(2)}, u32[]{:S(2)}) %collective-permute-start.17) | collective-permute-done | bytes 156704 | tf_op jit(solution)/shard_map/ppermute | solution.py:18
  (180 shorter events, 46.3 us)
Async XLA Ops:
  0.6 24.8 %copy-start = (f32[17]{0:T(128)S(1)}, f32[17]{0:T(128)}, u32[]{:S(2)}) copy-start(f32[17]{0:T(128)} %param.16) | copy-start | bytes 208
  1.4 64.5 %copy-start.3 = (f32[1,4,8,128]{3,2,1,0:T(8,128)}, f32[1,4,8,128]{3,2,1,0:T(8,128)S(1)}, u32[]{:S(2)}) copy-start(f32[1,4,8,128]{3,2,1,0:T(8,128)S(1)} %get-tuple-element.64) | copy-start | bytes 49156
  2.7 19.3 %copy-start.43 = (s32[4,73]{1,0:T(4,128)S(1)}, s32[4,73]{1,0:T(4,128)}, u32[]{:S(2)}) copy-start(s32[4,73]{1,0:T(4,128)} %param.17) | copy-start | bytes 3508
  3.7 57.7 %collective-permute-start = (f32[3,18,4,8,128]{4,3,2,1,0:T(8,128)}, f32[3,18,4,8,128]{4,3,2,1,0:T(8,128)}, u32[]{:S(2)}, u32[]{:S(2)}) collective-permute-start(f32[3,18,4,8,128]{4,3,2,1,0:T(8,128)} %pad_maximum_fusion.4), channel_id=1, source_target_pairs={{4,0},{8,4},{12,8},{16,12},{20,16},{24,20},{28,24},{32,28},{36,32}... | collective-permute-start | bytes 2654216 | tf_op jit(solution)/shard_map/ppermute | solution.py:21
  14.9 48.7 %collective-permute-start.1 = (f32[3,18,4,8,128]{4,3,2,1,0:T(8,128)}, f32[3,18,4,8,128]{4,3,2,1,0:T(8,128)}, u32[]{:S(2)}, u32[]{:S(2)}) collective-permute-start(f32[3,18,4,8,128]{4,3,2,1,0:T(8,128)} %pad_maximum_fusion.4), channel_id=1, source_target_pairs={{0,4},{4,8},{8,12},{12,16},{16,20},{20,24},{24,28},{28,32},{32,36}... | collective-permute-start | bytes 2654216 | tf_op jit(solution)/shard_map/ppermute | solution.py:18
  17.7 8.0 %collective-permute-start.2 = (f32[18,4,8,4]{3,2,1,0:T(8,128)}, f32[18,4,8,4]{3,2,1,0:T(8,128)S(1)}, u32[]{:S(2)}, u32[]{:S(2)}) collective-permute-start(f32[18,4,8,4]{3,2,1,0:T(8,128)} %get-tuple-element.56), channel_id=1, source_target_pairs={{2,0},{0,2},{3,1},{1,3},{6,4},{4,6},{7,5},{5,7},{10,8},{8,10},{11,... | collective-permute-start | bytes 27656 | tf_op jit(solution)/shard_map/ppermute | solution.py:21
  19.7 6.1 %collective-permute-start.3 = (f32[18,4,8,4]{3,2,1,0:T(8,128)}, f32[18,4,8,4]{3,2,1,0:T(8,128)}, u32[]{:S(2)}, u32[]{:S(2)}) collective-permute-start(f32[18,4,8,4]{3,2,1,0:T(8,128)} %get-tuple-element.55), channel_id=1, source_target_pairs={{0,2},{2,0},{1,3},{3,1},{4,6},{6,4},{5,7},{7,5},{8,10},{10,8},{9,1... | collective-permute-start | bytes 27656 | tf_op jit(solution)/shard_map/ppermute | solution.py:18
  27.2 26.2 %collective-permute-start.4 = (f32[18,4,4,136]{3,2,1,0:T(4,128)S(1)}, f32[18,4,4,136]{3,2,1,0:T(4,128)S(1)}, u32[]{:S(2)}, u32[]{:S(2)}) collective-permute-start(f32[18,4,4,136]{3,2,1,0:T(4,128)S(1)} %get-tuple-element.37), channel_id=1, source_target_pairs={{1,0},{0,1},{3,2},{2,3},{5,4},{4,5},{7,6},{6,7},{9,8},{8,9},{11,10... | collective-permute-start | bytes 470024 | tf_op jit(solution)/shard_map/ppermute | solution.py:21
  31.3 28.3 %collective-permute-start.5 = (f32[18,4,4,136]{3,2,1,0:T(4,128)S(1)}, f32[18,4,4,136]{3,2,1,0:T(4,128)S(1)}, u32[]{:S(2)}, u32[]{:S(2)}) collective-permute-start(f32[18,4,4,136]{3,2,1,0:T(4,128)S(1)} %get-tuple-element.38), channel_id=1, source_target_pairs={{0,1},{1,0},{2,3},{3,2},{4,5},{5,4},{6,7},{7,6},{8,9},{9,8},{10,11... | collective-permute-start | bytes 470024 | tf_op jit(solution)/shard_map/ppermute | solution.py:18
  33.3 32.7 %copy-start.11 = (f32[4,8,128]{2,1,0:T(8,128)}, f32[4,8,128]{2,1,0:T(8,128)S(1)}, u32[]{:S(2)}) copy-start(f32[4,8,128]{2,1,0:T(8,128)S(1)} %get-tuple-element.59) | copy-start | bytes 49156
  33.3 32.7 %copy-start.14 = (f32[4,8,128]{2,1,0:T(8,128)}, f32[4,8,128]{2,1,0:T(8,128)S(1)}, u32[]{:S(2)}) copy-start(f32[4,8,128]{2,1,0:T(8,128)S(1)} %get-tuple-element.60) | copy-start | bytes 49156
  33.3 32.7 %copy-start.17 = (f32[4,8,128]{2,1,0:T(8,128)}, f32[4,8,128]{2,1,0:T(8,128)S(1)}, u32[]{:S(2)}) copy-start(f32[4,8,128]{2,1,0:T(8,128)S(1)} %get-tuple-element.61) | copy-start | bytes 49156
  71.0 6.2 %collective-permute-start.6 = (f32[18,4,8,4]{3,2,1,0:T(8,128)S(1)}, f32[18,4,8,4]{3,2,1,0:T(8,128)S(1)}, u32[]{:S(2)}, u32[]{:S(2)}) collective-permute-start(f32[18,4,8,4]{3,2,1,0:T(8,128)S(1)} %get-tuple-element.48), channel_id=1, source_target_pairs={{2,0},{0,2},{3,1},{1,3},{6,4},{4,6},{7,5},{5,7},{10,8},{8,10},{11,... | collective-permute-start | bytes 27656 | tf_op jit(solution)/shard_map/ppermute | solution.py:21
  73.0 4.2 %collective-permute-start.7 = (f32[18,4,8,4]{3,2,1,0:T(8,128)S(1)}, f32[18,4,8,4]{3,2,1,0:T(8,128)S(1)}, u32[]{:S(2)}, u32[]{:S(2)}) collective-permute-start(f32[18,4,8,4]{3,2,1,0:T(8,128)S(1)} %get-tuple-element.47), channel_id=1, source_target_pairs={{0,2},{2,0},{1,3},{3,1},{4,6},{6,4},{5,7},{7,5},{8,10},{10,8},{9,1... | collective-permute-start | bytes 27656 | tf_op jit(solution)/shard_map/ppermute | solution.py:18
  77.7 11.8 %collective-permute-start.8 = (f32[18,4,4,136]{3,2,1,0:T(4,128)S(1)}, f32[18,4,4,136]{3,2,1,0:T(4,128)S(1)}, u32[]{:S(2)}, u32[]{:S(2)}) collective-permute-start(f32[18,4,4,136]{3,2,1,0:T(4,128)S(1)} %get-tuple-element.35), channel_id=1, source_target_pairs={{1,0},{0,1},{3,2},{2,3},{5,4},{4,5},{7,6},{6,7},{9,8},{8,9},{11,10... | collective-permute-start | bytes 470024 | tf_op jit(solution)/shard_map/ppermute | solution.py:21
  80.4 14.5 %collective-permute-start.9 = (f32[18,4,4,136]{3,2,1,0:T(4,128)S(1)}, f32[18,4,4,136]{3,2,1,0:T(4,128)S(1)}, u32[]{:S(2)}, u32[]{:S(2)}) collective-permute-start(f32[18,4,4,136]{3,2,1,0:T(4,128)S(1)} %get-tuple-element.36), channel_id=1, source_target_pairs={{0,1},{1,0},{2,3},{3,2},{4,5},{5,4},{6,7},{7,6},{8,9},{9,8},{10,11... | collective-permute-start | bytes 470024 | tf_op jit(solution)/shard_map/ppermute | solution.py:18
  99.6 6.2 %collective-permute-start.10 = (f32[18,4,8,4]{3,2,1,0:T(8,128)S(1)}, f32[18,4,8,4]{3,2,1,0:T(8,128)S(1)}, u32[]{:S(2)}, u32[]{:S(2)}) collective-permute-start(f32[18,4,8,4]{3,2,1,0:T(8,128)S(1)} %get-tuple-element.44), channel_id=1, source_target_pairs={{2,0},{0,2},{3,1},{1,3},{6,4},{4,6},{7,5},{5,7},{10,8},{8,10},{11,... | collective-permute-start | bytes 27656 | tf_op jit(solution)/shard_map/ppermute | solution.py:21
  101.6 4.3 %collective-permute-start.11 = (f32[18,4,8,4]{3,2,1,0:T(8,128)S(1)}, f32[18,4,8,4]{3,2,1,0:T(8,128)S(1)}, u32[]{:S(2)}, u32[]{:S(2)}) collective-permute-start(f32[18,4,8,4]{3,2,1,0:T(8,128)S(1)} %get-tuple-element.43), channel_id=1, source_target_pairs={{0,2},{2,0},{1,3},{3,1},{4,6},{6,4},{5,7},{7,5},{8,10},{10,8},{9,1... | collective-permute-start | bytes 27656 | tf_op jit(solution)/shard_map/ppermute | solution.py:18
  106.3 11.8 %collective-permute-start.12 = (f32[18,4,4,136]{3,2,1,0:T(4,128)S(1)}, f32[18,4,4,136]{3,2,1,0:T(4,128)S(1)}, u32[]{:S(2)}, u32[]{:S(2)}) collective-permute-start(f32[18,4,4,136]{3,2,1,0:T(4,128)S(1)} %get-tuple-element.33), channel_id=1, source_target_pairs={{1,0},{0,1},{3,2},{2,3},{5,4},{4,5},{7,6},{6,7},{9,8},{8,9},{11,10... | collective-permute-start | bytes 470024 | tf_op jit(solution)/shard_map/ppermute | solution.py:21
  109.0 14.5 %collective-permute-start.13 = (f32[18,4,4,136]{3,2,1,0:T(4,128)S(1)}, f32[18,4,4,136]{3,2,1,0:T(4,128)S(1)}, u32[]{:S(2)}, u32[]{:S(2)}) collective-permute-start(f32[18,4,4,136]{3,2,1,0:T(4,128)S(1)} %get-tuple-element.34), channel_id=1, source_target_pairs={{0,1},{1,0},{2,3},{3,2},{4,5},{5,4},{6,7},{7,6},{8,9},{9,8},{10,11... | collective-permute-start | bytes 470024 | tf_op jit(solution)/shard_map/ppermute | solution.py:18
  128.7 6.4 %collective-permute-start.14 = (f32[18,4,8,4]{3,2,1,0:T(8,128)S(1)}, f32[18,4,8,4]{3,2,1,0:T(8,128)S(1)}, u32[]{:S(2)}, u32[]{:S(2)}) collective-permute-start(f32[18,4,8,4]{3,2,1,0:T(8,128)S(1)} %get-tuple-element.40), channel_id=1, source_target_pairs={{2,0},{0,2},{3,1},{1,3},{6,4},{4,6},{7,5},{5,7},{10,8},{8,10},{11,... | collective-permute-start | bytes 27656 | tf_op jit(solution)/shard_map/ppermute | solution.py:21
  130.6 4.4 %collective-permute-start.15 = (f32[18,4,8,4]{3,2,1,0:T(8,128)S(1)}, f32[18,4,8,4]{3,2,1,0:T(8,128)S(1)}, u32[]{:S(2)}, u32[]{:S(2)}) collective-permute-start(f32[18,4,8,4]{3,2,1,0:T(8,128)S(1)} %get-tuple-element.39), channel_id=1, source_target_pairs={{0,2},{2,0},{1,3},{3,1},{4,6},{6,4},{5,7},{7,5},{8,10},{10,8},{9,1... | collective-permute-start | bytes 27656 | tf_op jit(solution)/shard_map/ppermute | solution.py:18
  135.5 11.8 %collective-permute-start.16 = (f32[18,4,4,136]{3,2,1,0:T(4,128)S(1)}, f32[18,4,4,136]{3,2,1,0:T(4,128)S(1)}, u32[]{:S(2)}, u32[]{:S(2)}) collective-permute-start(f32[18,4,4,136]{3,2,1,0:T(4,128)S(1)} %get-tuple-element.31), channel_id=1, source_target_pairs={{1,0},{0,1},{3,2},{2,3},{5,4},{4,5},{7,6},{6,7},{9,8},{8,9},{11,10... | collective-permute-start | bytes 470024 | tf_op jit(solution)/shard_map/ppermute | solution.py:21
  138.1 14.5 %collective-permute-start.17 = (f32[18,4,4,136]{3,2,1,0:T(4,128)S(1)}, f32[18,4,4,136]{3,2,1,0:T(4,128)S(1)}, u32[]{:S(2)}, u32[]{:S(2)}) collective-permute-start(f32[18,4,4,136]{3,2,1,0:T(4,128)S(1)} %get-tuple-element.32), channel_id=1, source_target_pairs={{0,1},{1,0},{2,3},{3,2},{4,5},{5,4},{6,7},{7,6},{8,9},{9,8},{10,11... | collective-permute-start | bytes 470024 | tf_op jit(solution)/shard_map/ppermute | solution.py:18
  (38 other events, 223.7 us)
where the time goes:
time: 158 us; the launch traced here: 157 us
  waiting for transfers between devices  57.7 us (37%)
  starting transfers between devices  54.3 us (34%)
  other arithmetic  25 us (16%)
  local copies, waits for them, and re-layouts  11 us (7%)
  matrix products  6.88 us (4%)
  between operations  2 us (1%)
    ppermute x9, waiting for transfers between devices, with_halo(): lax.ppermute(lax.slice_in_dim(block, 0, width, axis=dim), axis, backward)  35.3 us
    ppermute x9, starting transfers between devices, with_halo(): lax.ppermute(lax.slice_in_dim(block, 0, width, axis=dim), axis, backward)  30.9 us
    ppermute x9, starting transfers between devices, with_halo(): lax.ppermute(lax.slice_in_dim(block, block.shape[dim] - width, None, axis...  23.5 us
    ppermute x9, waiting for transfers between devices, with_halo(): lax.ppermute(lax.slice_in_dim(block, block.shape[dim] - width, None, axis...  22.4 us
    concatenate x9, other arithmetic, with_halo(): block = jnp.concatenate([low, block, high], axis=dim)  7.54 us
    sub x4, other arithmetic, tendency(): change = diffusion * laplace - transport  6.85 us
    dot_general x4, matrix products, combustion_source_terms(): jnp.tensordot(stoich, progress, axes=1, precision=lax.Precision.HIGHEST)  5.52 us
  transfers between devices with their start and end apart: 18, of which 8 were waited for; matrix products, arithmetic and copies ran while one was open for 11% of the time, Pallas kernels for 0%

commit v1 on v0

v1 whole, which is shorter than its diff:
```python
import functools

import jax
import jax.numpy as jnp
import numpy as np
from jax import lax
from jax.experimental import pallas as pl
from jax.experimental.pallas import tpu as pltpu
from jax.sharding import PartitionSpec as P

SPECIES = 17
FIELDS = 18
REACT = 73
CX = 4
CZ = 8
CY = 128
ROWS = FIELDS * CZ
LANES = CX * CY
QUAD = 4
QUADS = (FIELDS + QUAD - 1) // QUAD
QROWS = 640
CHUNKS = ((0, 8), (8, 16), (16, 18))

time_step = 0.125
first_coeffs = (4.0 / 5.0, -1.0 / 5.0, 4.0 / 105.0, -1.0 / 280.0)
second_coeffs = (8.0 / 5.0, -1.0 / 5.0, 8.0 / 315.0, -1.0 / 560.0)
center_coeff = -205.0 / 72.0

MESH = pl.DeviceIdType.MESH


FIRST_SCALE = 840.0
SECOND_SCALE = 5040.0
first_scaled = (672.0, -168.0, 32.0, -3.0)
second_scaled = (8064.0, -1008.0, 128.0, -9.0)


def weight(distance):
    size = abs(distance)
    if size == 0 or size > 4:
        return 0.0, 0.0
    sign = 1.0 if distance > 0 else -1.0
    return sign * first_coeffs[size - 1], second_coeffs[size - 1]


def scaled(distance):
    size = abs(distance)
    if size == 0 or size > 4:
        return 0.0, 0.0
    sign = 1.0 if distance > 0 else -1.0
    return sign * first_scaled[size - 1], second_scaled[size - 1]


def y_matrix():
    matrix = np.zeros((CY, 2 * CY), np.float32)
    for out in range(CY):
        for at in range(CY):
            matrix[at, out], matrix[at, CY + out] = scaled(at - out)
    return np.concatenate([matrix, matrix])


def edge_matrix():
    matrix = np.zeros((CY, 2 * CY), np.float32)
    for base in range(0, CY, 8):
        for at in range(8):
            for out in range(8):
                if (at < 4) != (out < 4):
                    first, second = scaled(at - out)
                    matrix[base + at, base + out] = first
                    matrix[base + at, CY + base + out] = second
    return np.concatenate([matrix, matrix])


def z_matrix():
    half = QUAD * CZ
    matrix = np.zeros((2 * half, 2 * half), np.float32)
    for slab in range(QUAD):
        for out in range(CZ):
            for step in range(-4, 5):
                at = out + step
                column = slab * CZ + at % CZ + (0 if 0 <= at < CZ else half)
                first, second = scaled(step)
                matrix[slab * CZ + out, column] += first
                matrix[half + slab * CZ + out, column] += second
    return np.concatenate([matrix, matrix], axis=1)


def split(value):
    high = value.astype(jnp.bfloat16)
    return high, (value - high.astype(jnp.float32)).astype(jnp.bfloat16)


def dot(left, right):
    return jnp.dot(left, right, preferred_element_type=jnp.float32)


def kernel(
    n_gx,
    conc, therm, veloc, table_h, logs_h, barriers_h, heats_h, kappas_h, ymat_h, emat_h, zmat_h,
    conc_out, therm_out,
    past, lev_a, lev_n, lev_c, vel, xhalo, xterm, state1, state2, state3, zhalo, ypack, yhalo,
    rate, local, result, qbuf, made, parts, near, dy, dz1, dz2, edge, kpack, vpack, nuk,
    ymat, emat, zmat, ymat_v, emat_v, zmat_v,
    table_s, logs, barriers, heats, kappas, table_v,
    past_sem, ld_sem, vel_send, swap_send, arrive, x_send, x_recv, z_send, z_recv, y_send, y_recv,
    o_send, o_recv,
):
    gx, gy, gz = lax.axis_index("gx"), lax.axis_index("gy"), lax.axis_index("gz")
    period = max(n_gx // 8, 1)

    def half_of(at):
        return lax.rem(lax.div(at, period), 2)

    mirrored = half_of(gx)
    moves = lax.rem(gy + gz + mirrored, 2) == 1

    def x_beside(at):
        flips = half_of(at) != mirrored
        return {
            "gx": at,
            "gy": jnp.where(flips, 1 - gy, gy),
            "gz": jnp.where(flips, 1 - gz, gz),
        }

    right = x_beside(lax.rem(gx + 1, n_gx))
    left = x_beside(lax.rem(gx + n_gx - 1, n_gx))
    z_partner = {"gx": gx, "gy": 1 - gy, "gz": gz}
    y_partner = {"gx": gx, "gy": gy, "gz": 1 - gz}
    opposite = {"gx": gx, "gy": 1 - gy, "gz": 1 - gz}

    def remote(src, dst, send, recv, where):
        return pltpu.make_async_remote_copy(
            src_ref=src, dst_ref=dst, send_sem=send, recv_sem=recv,
            device_id=where, device_id_type=MESH,
        )

    past_loads = []
    for chunk, (begin, end) in enumerate(CHUNKS):
        stop = min(end, SPECIES)
        copies = [(conc.at[0:2, begin:stop], past.at[:, begin:stop])]
        if end == FIELDS:
            copies.append((therm.at[0:2], past.at[:, SPECIES]))
        past_loads.append([
            pltpu.make_async_copy(src, dst, past_sem.at[chunk, at])
            for at, (src, dst) in enumerate(copies)
        ])
    shared = ((table_h, table_v), (ymat_h, ymat_v), (emat_h, emat_v), (zmat_h, zmat_v), (table_h, table_s),
              (logs_h, logs), (barriers_h, barriers), (heats_h, heats), (kappas_h, kappas))
    loads = [
        pltpu.make_async_copy(src, dst, ld_sem.at[at]) for at, (src, dst) in enumerate(shared)
    ]
    for copy in [copy for copies in past_loads for copy in copies] + loads:
        copy.start()

    barrier = pltpu.get_barrier_semaphore()
    for where in (left, right, z_partner, y_partner, opposite):
        pl.semaphore_signal(barrier, inc=1, device_id=where, device_id_type=MESH)

    def moved(level, chunk):
        begin, end = CHUNKS[chunk]
        if level == 0:
            return [(past.at[0, begin:end], lev_a.at[begin:end])]
        into = (lev_n, lev_c)[level - 1]
        stop = min(end, SPECIES)
        copies = [(conc.at[level, begin:stop], into.at[begin:stop])]
        if end == FIELDS:
            copies.append((therm.at[level], into.at[SPECIES]))
        return copies

    def swaps(level, chunk):
        return [
            remote(src, dst, swap_send.at[level, chunk, at], arrive.at[level, chunk, at], opposite)
            for at, (src, dst) in enumerate(moved(level, chunk))
        ]

    def own(level, chunk):
        return [
            pltpu.make_async_copy(src, dst, arrive.at[level, chunk, at])
            for at, (src, dst) in enumerate(moved(level, chunk))
        ]

    def placed(level, chunk):
        for at, (src, dst) in enumerate(moved(level, chunk)):
            pltpu.make_async_copy(dst, dst, arrive.at[level, chunk, at]).wait()

    vel_swap = remote(veloc, vel, vel_send.at[0], vel_send.at[1], opposite)
    vel_own = pltpu.make_async_copy(veloc, vel, vel_send.at[1])

    levels = (lev_a, lev_n, lev_c)

    def x_copies(level, chunk, source=None):
        begin, end = CHUNKS[chunk]
        src = (levels[level] if source is None else source).at[begin:end]
        return [
            remote(
                src, xhalo.at[level, side, begin:end],
                x_send.at[level, side, chunk], x_recv.at[level, side, chunk], where,
            )
            for side, where in ((0, right), (1, left))
        ]

    def delay(chunk):
        for copy in past_loads[chunk]:
            copy.wait()

        def one(field, carry):
            past[0, field] = 2.0 * past[1, field] - past[0, field]
            return carry

        lax.fori_loop(*CHUNKS[chunk], one, 0, unroll=2)

    def start(copies):
        for copy in copies:
            copy.start()

    stays = jnp.logical_not(moves)
    chunks = range(len(CHUNKS))

    pl.semaphore_wait(barrier, 5)

    @pl.when(stays)
    def _():
        vel_own.start()
        for chunk in chunks:
            start(own(2, chunk))
        for chunk in chunks:
            delay(chunk)
            start(x_copies(0, chunk, past.at[0]))
        for chunk in chunks:
            start(x_copies(1, chunk, past.at[1]))

    @pl.when(moves)
    def _():
        vel_swap.start()
        for chunk in chunks:
            delay(chunk)
            start(swaps(0, chunk))
        for chunk in chunks:
            start(swaps(2, chunk))
        for chunk in chunks:
            start(swaps(1, chunk))

    for load in loads:
        load.wait()
    for matrix, into in ((ymat_v, ymat), (emat_v, emat), (zmat_v, zmat)):
        into[...] = matrix[...].astype(jnp.bfloat16)

    filler = jnp.full((4, CY - REACT), 31.0, jnp.float32)
    members = jnp.concatenate([table_v[...].astype(jnp.float32), filler], axis=1)
    members = jnp.concatenate([members, jnp.zeros((12, CY), jnp.float32)], axis=0)
    column = lax.broadcasted_iota(jnp.int32, (CY, 2 * QROWS), 1)
    column = jnp.where(column >= QROWS, column - QROWS, column)
    reaction = lax.broadcasted_iota(jnp.int32, (CY, 2 * QROWS), 0)
    spread = jnp.where(lax.shift_right_logical(column, 3) == reaction, 1.0, 0.0)
    members = dot(members.astype(jnp.bfloat16), spread.astype(jnp.bfloat16))
    level_z = lax.broadcasted_iota(jnp.int32, (CZ, 2 * QROWS), 0)
    same_z = (lax.broadcasted_iota(jnp.int32, (CZ, 2 * QROWS), 1) & 7) == level_z
    for species in range(0, FIELDS, 2):
        both = []
        for at in (species, species + 1):
            total = jnp.zeros((1, 2 * QROWS), jnp.float32)
            if at < SPECIES:
                for which, sign in ((0, -1.0), (1, -1.0), (2, 1.0), (3, 1.0)):
                    total = total + jnp.where(members[which : which + 1] == at, sign, 0.0)
            both.append(jnp.where(same_z, total, 0.0))
        rows = slice(CZ * species, CZ * species + 2 * CZ)
        nuk[rows, :] = jnp.concatenate(both, axis=0).astype(jnp.bfloat16)
    filled = (REACT + 1) * CZ
    for begin in (filled, QROWS + filled):
        qbuf[begin : begin + QROWS - filled, :] = jnp.zeros((QROWS - filled, LANES), jnp.bfloat16)

    lane_block = lax.broadcasted_iota(jnp.int32, (CZ, CY), 1) // 8
    lane = lax.broadcasted_iota(jnp.int32, (CZ, CY), 1)
    at_edge = jnp.logical_or(lane < 4, lane >= CY - 4)
    for quad in range(QUADS):
        packed = jnp.zeros((CZ, CY), jnp.float32)
        for slab in range(min(QUAD, FIELDS - QUAD * quad)):
            packed = jnp.where(
                lane_block // CX == slab, kappas[0, QUAD * quad + slab], packed
            )
        kpack[quad] = packed * (1.0 / SECOND_SCALE)

    @pl.when(moves)
    def _():
        for chunk in chunks:
            placed(0, chunk)
            start(x_copies(0, chunk))

    def z_copy(k, state, chunk):
        begin, end = CHUNKS[chunk]
        return remote(
            state.at[begin:end], zhalo.at[k, begin:end], z_send.at[k, chunk], z_recv.at[k, chunk],
            z_partner,
        )

    def y_copy(k):
        return remote(ypack.at[k], yhalo.at[k], y_send.at[k], y_recv.at[k], y_partner)

    def pack(columns):
        packed = jnp.zeros((CZ, CY), jnp.float32)
        for at, value in enumerate(columns):
            packed = jnp.where(lane_block == at, pltpu.roll(value, (8 * at + 4) % CY, 1), packed)
        return packed

    def send_borders(k, state, chunk):
        z_copy(k, state, chunk).start()
        begin, end = CHUNKS[chunk]
        for first in range(begin, end, QUAD):
            fields = range(first, min(first + QUAD, end))
            ypack[k, first // QUAD] = pack([state[f, x] for f in fields for x in range(CX)])
        if end == FIELDS:
            y_copy(k).start()

    def reactions(state):
        total = state[0]
        for species in range(1, SPECIES):
            total = total + state[species]
        state[FIELDS] = total * (1.0 / SPECIES)
        inverse = 1.0 / state[SPECIES]

        def two(pair, carry):
            both = []
            for at in range(2):
                j = jnp.minimum(2 * pair + at, REACT - 1)
                first, second = table_s[0, j], table_s[1, j]
                first = jnp.where(first == SPECIES, FIELDS, first)
                second = jnp.where(second == SPECIES, FIELDS, second)
                speed = jnp.exp(logs[0, j] - barriers[0, j] * inverse)
                both.append(speed * state[first] * state[second])
            begin = pl.multiple_of(16 * pair, 16)
            for x in range(CX):
                high, low = split(jnp.concatenate([both[0][x], both[1][x]], axis=0))
                lanes = slice(CY * x, CY * x + CY)
                qbuf[pl.ds(begin, 16), lanes] = high
                qbuf[pl.ds(QROWS + begin, 16), lanes] = low
            return carry

        lax.fori_loop(0, (REACT + 1) // 2, two, 0, unroll=2)

    def in_parts(source, into):
        for f in range(0, FIELDS, 2):
            for x in range(CX):
                value = jnp.concatenate([source[f, x], source[f + 1, x]], axis=0)
                into[x, CZ * f : CZ * f + 16, 0:CY], into[x, CZ * f : CZ * f + 16, CY:] = split(
                    value
                )

    def transport(k, state, finish, done=None):
        in_parts(state, parts)
        made[...] = dot(nuk[...], qbuf[...]).reshape(FIELDS, CZ, LANES)
        for x in range(CX):
            dy[x] = dot(parts[x], ymat[...]).reshape(FIELDS, CZ, 2 * CY)
        for chunk in chunks:
            z_copy(k, state, chunk).wait_recv()
        in_parts(zhalo.at[k], near)
        for first in (0, 4, 8, 12, 14):
            rows = slice(CZ * first, CZ * (first + QUAD))
            for x in range(0, CX, 2):
                sides = []
                for at in (x, x + 1):
                    sides.append(jnp.concatenate(
                        [parts[at, rows, 0:CY], near[at, rows, 0:CY],
                         parts[at, rows, CY:], near[at, rows, CY:]], axis=0,
                    ))
                out = dot(zmat[...], jnp.concatenate(sides, axis=1))
                lanes = slice(CY * x, CY * x + 2 * CY)
                dz1[first : first + QUAD, :, lanes] = out[: QUAD * CZ].reshape(QUAD, CZ, 2 * CY)
                dz2[first : first + QUAD, :, lanes] = out[QUAD * CZ :].reshape(QUAD, CZ, 2 * CY)
        y_copy(k).wait_recv()
        value = jnp.concatenate(
            [yhalo[k].reshape(QUADS * CZ, CY), jnp.zeros((CZ, CY), jnp.float32)], axis=0
        )
        out = dot(jnp.concatenate(split(value), axis=1), emat[...])
        for quad in range(QUADS):
            part = out[CZ * quad : CZ * quad + CZ]
            edge[quad] = kpack[quad] * part[:, CY:] - vpack[...] * part[:, 0:CY]

        def one(f, x, packed, at, source):
            values = [state[f, q] for q in range(CX)]
            grad, curv = None, (3.0 * center_coeff) * values[x]
            for q in range(CX):
                if q != x:
                    first, second = weight(q - x)
                    curv = curv + second * values[q]
                    grad = first * values[q] if grad is None else grad + first * values[q]
            lanes = slice(CY * x, CY * x + CY)
            curv = curv + (1.0 / SECOND_SCALE) * (dy[x, f, :, CY:] + dz2[f, :, lanes])
            along = vel[0, x] * grad + vel[1, x] * dy[x, f, :, 0:CY] + vel[2, x] * dz1[f, :, lanes]
            border = pltpu.roll(packed, (CY - (8 * at + 4)) % CY, 1)
            source = source + jnp.where(at_edge, border, 0.0)
            finish(f, x, kappas[0, f] * curv - along + source)

        def quad_of_fields(quad, release, fields=QUAD):
            release = list(release)
            packed = edge[quad]
            for slab in range(fields):
                f = QUAD * quad + slab
                for x in range(CX):
                    at = slab * CX + x
                    if slab == 1 and fields == 2:
                        one(f, x, packed, at, release[x])
                        continue
                    source = made[f, :, CY * x : CY * x + CY]
                    release[x] = release[x] + heats[0, f] * source
                    one(f, x, packed, at, source)
            return tuple(release)

        release = (jnp.zeros((CZ, CY), jnp.float32),) * CX
        for chunk, (begin, end) in enumerate(CHUNKS):
            release = lax.fori_loop(begin // QUAD, end // QUAD, quad_of_fields, release)
            if end == FIELDS:
                quad_of_fields(QUADS - 1, release, fields=2)
            if done is not None:
                done(chunk)

    def x_halo(level, make, done):
        def one(f, carry):
            before = [xhalo[level, 0, f, q] for q in range(CX)]
            after = [xhalo[level, 1, f, q] for q in range(CX)]
            for x in range(CX):
                grad = curv = None
                for q in range(CX):
                    for value, distance in ((before[q], q - 4 - x), (after[q], q + 4 - x)):
                        first, second = weight(distance)
                        if second == 0.0:
                            continue
                        grad = first * value if grad is None else grad + first * value
                        curv = second * value if curv is None else curv + second * value
                make(f, x, kappas[0, f] * curv - vel[0, x] * grad)
            return carry

        for chunk in chunks:
            for copy in x_copies(level, chunk):
                copy.wait_recv()
            lax.fori_loop(*CHUNKS[chunk], one, 0, unroll=2)
            done(chunk)

    def keep(f, x, value):
        local[f, x] = value

    for chunk in chunks:
        placed(2, chunk)
        send_borders(0, lev_c, chunk)
    reactions(lev_c)

    @pl.when(stays)
    def _():
        for chunk in chunks:
            start(x_copies(2, chunk))

    @pl.when(moves)
    def _():
        for chunk in chunks:
            placed(1, chunk)
            start(x_copies(1, chunk))

    vel_own.wait()
    for x in range(CX):
        vel[1, x] = vel[1, x] * (1.0 / FIRST_SCALE)
        vel[2, x] = vel[2, x] * (1.0 / FIRST_SCALE)
    vpack[...] = pack([vel[1, x] for x in range(CX)] * QUAD)
    transport(0, lev_c, keep)

    @pl.when(moves)
    def _():
        for chunk in chunks:
            start(x_copies(2, chunk))

    def make(f, x, share):
        xterm[0, f, x] = share
        value = local[f, x] + share
        rate[f, x] = value
        state1[f, x] = lev_c[f, x] + time_step * value

    x_halo(0, make, lambda chunk: send_borders(1, state1, chunk))

    reactions(state1)
    transport(1, state1, keep)

    def make(f, x, share):
        xterm[1, f, x] = share
        value = local[f, x] + 2.0 * xterm[0, f, x] - share
        state2[f, x] = lev_c[f, x] + 0.5 * time_step * (rate[f, x] + value)

    x_halo(1, make, lambda chunk: send_borders(2, state2, chunk))

    reactions(state2)
    transport(2, state2, keep)

    def make(f, x, late):
        before = xterm[1, f, x]
        value = local[f, x] + 2.0 * late - before
        state3[f, x] = state2[f, x] + time_step * value
        rate[f, x] = value + 3.0 * late - 2.0 * before

    x_halo(2, make, lambda chunk: send_borders(3, state3, chunk))

    reactions(state3)

    def last(f, x, value):
        result[f, x] = state2[f, x] + 0.5 * time_step * (rate[f, x] + value)

    def outs(chunk):
        begin, end = CHUNKS[chunk]
        stop = min(end, SPECIES)
        copies = [(result.at[begin:stop], conc_out.at[begin:stop])]
        if end == FIELDS:
            copies.append((result.at[SPECIES], therm_out))
        return copies

    def out_swaps(chunk):
        return [
            remote(src, dst, o_send.at[chunk, at], o_recv.at[chunk, at], opposite)
            for at, (src, dst) in enumerate(outs(chunk))
        ]

    def out_own(chunk):
        return [
            pltpu.make_async_copy(src, dst, o_recv.at[chunk, at])
            for at, (src, dst) in enumerate(outs(chunk))
        ]

    def done(chunk):
        @pl.when(moves)
        def _():
            start(out_swaps(chunk))

        @pl.when(stays)
        def _():
            start(out_own(chunk))

    transport(3, state3, last, done)

    for level in range(3):
        for chunk in chunks:
            for copy in x_copies(level, chunk):
                copy.wait_send()
    for k, state in enumerate((lev_c, state1, state2, state3)):
        for chunk in chunks:
            z_copy(k, state, chunk).wait_send()
        y_copy(k).wait_send()

    @pl.when(moves)
    def _():
        vel_swap.wait_send()
        for chunk in chunks:
            for copy in swaps(0, chunk) + swaps(1, chunk) + swaps(2, chunk) + out_swaps(chunk):
                copy.wait_send()

    for chunk in chunks:
        for at, (src, dst) in enumerate(outs(chunk)):
            pltpu.make_async_copy(dst, dst, o_recv.at[chunk, at]).wait()


def local(
    concentration_levels,
    thermal_levels,
    fluid_velocity,
    diffusivity,
    natural_logged_prefactors,
    energy_barrier_kelvin,
    enthalpy_yield_per_mole,
    stoichiometric_member_table,
):
    n_gx = lax.axis_size("gx")
    any_space = pl.BlockSpec(memory_space=pl.ANY)
    f32, bf16 = jnp.float32, jnp.bfloat16
    block = (FIELDS, CX, CZ, CY)
    wide = (FIELDS + 1, CX, CZ, CY)
    parts = len(CHUNKS)
    dma = pltpu.SemaphoreType.DMA
    scratch = [
        pltpu.VMEM((2,) + block, f32),
        pltpu.VMEM(block, f32),
        pltpu.VMEM(block, f32),
        pltpu.VMEM(wide, f32),
        pltpu.VMEM((3, CX, CZ, CY), f32),
        pltpu.VMEM((3, 2) + block, f32),
        pltpu.VMEM((2,) + block, f32),
        pltpu.VMEM(wide, f32),
        pltpu.VMEM(wide, f32),
        pltpu.VMEM(wide, f32),
        pltpu.VMEM((4,) + block, f32),
        pltpu.VMEM((4, QUADS, CZ, CY), f32),
        pltpu.VMEM((4, QUADS, CZ, CY), f32),
        pltpu.VMEM(block, f32),
        pltpu.VMEM(block, f32),
        pltpu.VMEM(block, f32),
        pltpu.VMEM((2 * QROWS, LANES), bf16),
        pltpu.VMEM((FIELDS, CZ, LANES), f32),
        pltpu.VMEM((CX, ROWS, 2 * CY), bf16),
        pltpu.VMEM((CX, ROWS, 2 * CY), bf16),
        pltpu.VMEM((CX, FIELDS, CZ, 2 * CY), f32),
        pltpu.VMEM((FIELDS, CZ, LANES), f32),
        pltpu.VMEM((FIELDS, CZ, LANES), f32),
        pltpu.VMEM((QUADS, CZ, CY), f32),
        pltpu.VMEM((QUADS, CZ, CY), f32),
        pltpu.VMEM((CZ, CY), f32),
        pltpu.VMEM((ROWS, 2 * QROWS), bf16),
        pltpu.VMEM((2 * CY, 2 * CY), bf16),
        pltpu.VMEM((2 * CY, 2 * CY), bf16),
        pltpu.VMEM((2 * QUAD * CZ, 4 * QUAD * CZ), bf16),
        pltpu.VMEM((2 * CY, 2 * CY), f32),
        pltpu.VMEM((2 * CY, 2 * CY), f32),
        pltpu.VMEM((2 * QUAD * CZ, 4 * QUAD * CZ), f32),
        pltpu.SMEM((4, REACT), jnp.int32),
        pltpu.SMEM((1, REACT), f32),
        pltpu.SMEM((1, REACT), f32),
        pltpu.SMEM((1, SPECIES), f32),
        pltpu.SMEM((1, FIELDS), f32),
        pltpu.VMEM((4, REACT), jnp.int32),
        dma((parts, 2)),
        dma((9,)),
        dma((2,)),
        dma((3, parts, 2)),
        dma((3, parts, 2)),
        dma((3, 2, parts)),
        dma((3, 2, parts)),
        dma((4, parts)),
        dma((4, parts)),
        dma((4,)),
        dma((4,)),
        dma((parts, 2)),
        dma((parts, 2)),
    ]
    return pl.pallas_call(
        functools.partial(kernel, n_gx),
        out_shape=(
            jax.ShapeDtypeStruct((SPECIES, CX, CZ, CY), f32),
            jax.ShapeDtypeStruct((CX, CZ, CY), f32),
        ),
        in_specs=[any_space] * 11,
        out_specs=(any_space, any_space),
        scratch_shapes=scratch,
        compiler_params=pltpu.CompilerParams(
            collective_id=0, has_side_effects=True, vmem_limit_bytes=64 * 1024 * 1024
        ),
    )(
        concentration_levels,
        thermal_levels,
        fluid_velocity,
        stoichiometric_member_table,
        natural_logged_prefactors[None],
        energy_barrier_kelvin[None],
        enthalpy_yield_per_mole[None],
        diffusivity[None],
        jnp.asarray(y_matrix()),
        jnp.asarray(edge_matrix()),
        jnp.asarray(z_matrix()),
    )


def solution(mesh):
    in_specs = (
        P(None, None, "gx", "gz", "gy"),
        P(None, "gx", "gz", "gy"),
        P(None, "gx", "gz", "gy"),
        P(),
        P(),
        P(),
        P(),
        P(),
    )
    out_specs = (P(None, "gx", "gz", "gy"), P("gx", "gz", "gy"))
    return jax.shard_map(local, mesh=mesh, in_specs=in_specs, out_specs=out_specs, check_vma=False)
```

time: 158 us -> 50.6 us (0.32)
  the two profiles are of different devices: /device:TPU:16 before, /device:TPU:1 now
where the time goes in v1:
time: 50.6 us; the launch traced here: 50.5 us
  Pallas kernels  47.5 us (94%)
  local copies, waits for them, and re-layouts  2.3 us (5%)
  between operations  0.65 us (1%)
    pallas_call x1, Pallas kernels, local(): pl.pallas_call(functools.partial(kernel, n_gx), out_shape=(jax.ShapeDtype...  47.5 us
    unnamed x4, local copies, waits for them, and re-layouts  2.3 us

profile of v1, /device:TPU:1, one launch (start us, length us, event | category | flops | bytes accessed | tf_op | source)
XLA Modules:
  0.0 50.5 jit_solution(3901639386561657479)
XLA Ops:
  0.6 47.5 %shard_map.122 = (f32[17,4,8,128]{3,2,1,0:T(8,128)}, f32[4,8,128]{2,1,0:T(8,128)}) custom-call(f32[3,17,4,8,128]{4,3,2,1,0:T(8,128)} %conc.1, f32[3,4,8,128]{3,2,1,0:T(8,128)} %therm.1, f32[3,4,8,128]{3,2,1,0:T(8,128)} %veloc.1, s32[4,73]{1,0:T(4,128)} %table_h.1, f32[1,73]{1,0:T(1,128)} %bitcast.4, f32[1,73]{1,0:T(1,128)} %bitcast.5, f32[1,17]{1,0:T(1,128)} %bitcast.6, ...), custom_call_target="tpu_custom_call" | custom-call | tf_op jit(solution)/shard_map/pallas_call | solution.py:626
  48.2 0.0 copy-start
  48.2 1.7 %copy.15 = f32[17,4,8,128]{3,2,1,0:T(8,128)} copy(f32[17,4,8,128]{3,2,1,0:T(8,128)} %get-tuple-element.4) | data formatting | bytes 557056
  49.9 0.0 copy-done
  49.9 0.6 %copy.16 = f32[4,8,128]{2,1,0:T(8,128)} copy(f32[4,8,128]{2,1,0:T(8,128)S(1)} %copy-done) | data formatting | bytes 32768
Async XLA Ops:
  48.2 1.7 %copy-start = (f32[4,8,128]{2,1,0:T(8,128)S(1)}, f32[4,8,128]{2,1,0:T(8,128)}, u32[]{:S(2)}) copy-start(f32[4,8,128]{2,1,0:T(8,128)} %get-tuple-element.5) | copy-start | bytes 49156

commit v2 on v1

--- a/solution.py
+++ b/solution.py
@@ -97,12 +97,12 @@
 def kernel(
     n_gx,
     conc, therm, veloc, table_h, logs_h, barriers_h, heats_h, kappas_h, ymat_h, emat_h, zmat_h,
-    conc_out, therm_out,
+    next_out,
     past, lev_a, lev_n, lev_c, vel, xhalo, xterm, state1, state2, state3, zhalo, ypack, yhalo,
     rate, local, result, qbuf, made, parts, near, dy, dz1, dz2, edge, kpack, vpack, nuk,
     ymat, emat, zmat, ymat_v, emat_v, zmat_v,
     table_s, logs, barriers, heats, kappas, table_v,
-    past_sem, ld_sem, vel_send, swap_send, arrive, x_send, x_recv, z_send, z_recv, y_send, y_recv,
+    vel_near, past_sem, ld_sem, vel_send, swap_send, arrive, x_send, x_recv, z_send, z_recv, y_send, y_recv,
     o_send, o_recv,
 ):
     gx, gy, gz = lax.axis_index("gx"), lax.axis_index("gy"), lax.axis_index("gz")
@@ -137,15 +137,16 @@
     past_loads = []
     for chunk, (begin, end) in enumerate(CHUNKS):
         stop = min(end, SPECIES)
-        copies = [(conc.at[0:2, begin:stop], past.at[:, begin:stop])]
+        copies = [(conc.at[:, begin:stop], past.at[:, begin:stop])]
         if end == FIELDS:
-            copies.append((therm.at[0:2], past.at[:, SPECIES]))
+            copies.append((therm, past.at[:, SPECIES]))
         past_loads.append([
             pltpu.make_async_copy(src, dst, past_sem.at[chunk, at])
             for at, (src, dst) in enumerate(copies)
         ])
     shared = ((table_h, table_v), (ymat_h, ymat_v), (emat_h, emat_v), (zmat_h, zmat_v), (table_h, table_s),
-              (logs_h, logs), (barriers_h, barriers), (heats_h, heats), (kappas_h, kappas))
+              (logs_h, logs), (barriers_h, barriers), (heats_h, heats), (kappas_h, kappas),
+              (veloc, vel_near))
     loads = [
         pltpu.make_async_copy(src, dst, ld_sem.at[at]) for at, (src, dst) in enumerate(shared)
     ]
@@ -158,33 +159,22 @@
 
     def moved(level, chunk):
         begin, end = CHUNKS[chunk]
-        if level == 0:
-            return [(past.at[0, begin:end], lev_a.at[begin:end])]
-        into = (lev_n, lev_c)[level - 1]
-        stop = min(end, SPECIES)
-        copies = [(conc.at[level, begin:stop], into.at[begin:stop])]
-        if end == FIELDS:
-            copies.append((therm.at[level], into.at[SPECIES]))
-        return copies
-
-    def swaps(level, chunk):
-        return [
-            remote(src, dst, swap_send.at[level, chunk, at], arrive.at[level, chunk, at], opposite)
-            for at, (src, dst) in enumerate(moved(level, chunk))
-        ]
+        return past.at[level, begin:end], (lev_a, lev_n, lev_c)[level].at[begin:end]
+
+    def swap(level, chunk):
+        src, dst = moved(level, chunk)
+        return remote(src, dst, swap_send.at[level, chunk], arrive.at[level, chunk], opposite)
 
     def own(level, chunk):
-        return [
-            pltpu.make_async_copy(src, dst, arrive.at[level, chunk, at])
-            for at, (src, dst) in enumerate(moved(level, chunk))
-        ]
+        src, dst = moved(level, chunk)
+        return pltpu.make_async_copy(src, dst, arrive.at[level, chunk])
 
     def placed(level, chunk):
-        for at, (src, dst) in enumerate(moved(level, chunk)):
-            pltpu.make_async_copy(dst, dst, arrive.at[level, chunk, at]).wait()
-
-    vel_swap = remote(veloc, vel, vel_send.at[0], vel_send.at[1], opposite)
-    vel_own = pltpu.make_async_copy(veloc, vel, vel_send.at[1])
+        src, dst = moved(level, chunk)
+        pltpu.make_async_copy(dst, dst, arrive.at[level, chunk]).wait()
+
+    vel_swap = remote(vel_near, vel, vel_send.at[0], vel_send.at[1], opposite)
+    vel_own = pltpu.make_async_copy(vel_near, vel, vel_send.at[1])
 
     levels = (lev_a, lev_n, lev_c)
 
@@ -216,32 +206,38 @@
     stays = jnp.logical_not(moves)
     chunks = range(len(CHUNKS))
 
+    for chunk in chunks:
+        delay(chunk)
+    loads[-1].wait()
     pl.semaphore_wait(barrier, 5)
 
     @pl.when(stays)
     def _():
         vel_own.start()
         for chunk in chunks:
-            start(own(2, chunk))
-        for chunk in chunks:
-            delay(chunk)
+            own(2, chunk).start()
+        for chunk in chunks:
             start(x_copies(0, chunk, past.at[0]))
-        for chunk in chunks:
-            start(x_copies(1, chunk, past.at[1]))
 
     @pl.when(moves)
     def _():
+        for chunk in chunks:
+            swap(0, chunk).start()
         vel_swap.start()
-        for chunk in chunks:
-            delay(chunk)
-            start(swaps(0, chunk))
-        for chunk in chunks:
-            start(swaps(2, chunk))
-        for chunk in chunks:
-            start(swaps(1, chunk))
-
-    for load in loads:
+        for level in (2, 1):
+            for chunk in chunks:
+                swap(level, chunk).start()
+
+    for load in loads[:-1]:
         load.wait()
+
+    def place_of_mean(j, carry):
+        for side in range(2):
+            member = table_s[side, j]
+            table_s[side, j] = jnp.where(member == SPECIES, FIELDS, member)
+        return carry
+
+    lax.fori_loop(0, REACT, place_of_mean, 0)
     for matrix, into in ((ymat_v, ymat), (emat_v, emat), (zmat_v, zmat)):
         into[...] = matrix[...].astype(jnp.bfloat16)
 
@@ -323,8 +319,6 @@
             for at in range(2):
                 j = jnp.minimum(2 * pair + at, REACT - 1)
                 first, second = table_s[0, j], table_s[1, j]
-                first = jnp.where(first == SPECIES, FIELDS, first)
-                second = jnp.where(second == SPECIES, FIELDS, second)
                 speed = jnp.exp(logs[0, j] - barriers[0, j] * inverse)
                 both.append(speed * state[first] * state[second])
             begin = pl.multiple_of(16 * pair, 16)
@@ -335,32 +329,30 @@
                 qbuf[pl.ds(QROWS + begin, 16), lanes] = low
             return carry
 
-        lax.fori_loop(0, (REACT + 1) // 2, two, 0, unroll=2)
+        lax.fori_loop(0, (REACT + 1) // 2, two, 0, unroll=4)
 
     def in_parts(source, into):
         for f in range(0, FIELDS, 2):
             for x in range(CX):
+                rows = slice(ROWS * x + CZ * f, ROWS * x + CZ * f + 16)
                 value = jnp.concatenate([source[f, x], source[f + 1, x]], axis=0)
-                into[x, CZ * f : CZ * f + 16, 0:CY], into[x, CZ * f : CZ * f + 16, CY:] = split(
-                    value
-                )
+                into[rows, 0:CY], into[rows, CY:] = split(value)
 
     def transport(k, state, finish, done=None):
+        made[...] = dot(nuk[...], qbuf[...]).reshape(FIELDS, CZ, LANES)
         in_parts(state, parts)
-        made[...] = dot(nuk[...], qbuf[...]).reshape(FIELDS, CZ, LANES)
-        for x in range(CX):
-            dy[x] = dot(parts[x], ymat[...]).reshape(FIELDS, CZ, 2 * CY)
         for chunk in chunks:
             z_copy(k, state, chunk).wait_recv()
+        dy[...] = dot(parts[...], ymat[...]).reshape(CX, FIELDS, CZ, 2 * CY)
         in_parts(zhalo.at[k], near)
         for first in (0, 4, 8, 12, 14):
-            rows = slice(CZ * first, CZ * (first + QUAD))
             for x in range(0, CX, 2):
                 sides = []
                 for at in (x, x + 1):
+                    rows = slice(ROWS * at + CZ * first, ROWS * at + CZ * (first + QUAD))
                     sides.append(jnp.concatenate(
-                        [parts[at, rows, 0:CY], near[at, rows, 0:CY],
-                         parts[at, rows, CY:], near[at, rows, CY:]], axis=0,
+                        [parts[rows, 0:CY], near[rows, 0:CY], parts[rows, CY:], near[rows, CY:]],
+                        axis=0,
                     ))
                 out = dot(zmat[...], jnp.concatenate(sides, axis=1))
                 lanes = slice(CY * x, CY * x + 2 * CY)
@@ -406,12 +398,15 @@
             return tuple(release)
 
         release = (jnp.zeros((CZ, CY), jnp.float32),) * CX
+        if done is None:
+            release = lax.fori_loop(0, QUADS - 1, quad_of_fields, release)
+            quad_of_fields(QUADS - 1, release, fields=2)
+            return
         for chunk, (begin, end) in enumerate(CHUNKS):
             release = lax.fori_loop(begin // QUAD, end // QUAD, quad_of_fields, release)
             if end == FIELDS:
                 quad_of_fields(QUADS - 1, release, fields=2)
-            if done is not None:
-                done(chunk)
+            done(chunk)
 
     def x_halo(level, make, done):
         def one(f, carry):
@@ -432,7 +427,7 @@
         for chunk in chunks:
             for copy in x_copies(level, chunk):
                 copy.wait_recv()
-            lax.fori_loop(*CHUNKS[chunk], one, 0, unroll=2)
+            lax.fori_loop(*CHUNKS[chunk], one, 0, unroll=4 if chunk < 2 else 2)
             done(chunk)
 
     def keep(f, x, value):
@@ -441,18 +436,14 @@
     for chunk in chunks:
         placed(2, chunk)
         send_borders(0, lev_c, chunk)
-    reactions(lev_c)
 
     @pl.when(stays)
     def _():
-        for chunk in chunks:
-            start(x_copies(2, chunk))
-
-    @pl.when(moves)
-    def _():
-        for chunk in chunks:
-            placed(1, chunk)
-            start(x_copies(1, chunk))
+        for level in (1, 2):
+            for chunk in chunks:
+                start(x_copies(level, chunk, past.at[level]))
+
+    reactions(lev_c)
 
     vel_own.wait()
     for x in range(CX):
@@ -464,6 +455,9 @@
     @pl.when(moves)
     def _():
         for chunk in chunks:
+            placed(1, chunk)
+            start(x_copies(1, chunk))
+        for chunk in chunks:
             start(x_copies(2, chunk))
 
     def make(f, x, share):
@@ -502,32 +496,24 @@
 
     def outs(chunk):
         begin, end = CHUNKS[chunk]
-        stop = min(end, SPECIES)
-        copies = [(result.at[begin:stop], conc_out.at[begin:stop])]
-        if end == FIELDS:
-            copies.append((result.at[SPECIES], therm_out))
-        return copies
-
-    def out_swaps(chunk):
-        return [
-            remote(src, dst, o_send.at[chunk, at], o_recv.at[chunk, at], opposite)
-            for at, (src, dst) in enumerate(outs(chunk))
-        ]
+        return result.at[begin:end], next_out.at[begin:end]
+
+    def out_swap(chunk):
+        src, dst = outs(chunk)
+        return remote(src, dst, o_send.at[chunk], o_recv.at[chunk], opposite)
 
     def out_own(chunk):
-        return [
-            pltpu.make_async_copy(src, dst, o_recv.at[chunk, at])
-            for at, (src, dst) in enumerate(outs(chunk))
-        ]
+        src, dst = outs(chunk)
+        return pltpu.make_async_copy(src, dst, o_recv.at[chunk])
 
     def done(chunk):
         @pl.when(moves)
         def _():
-            start(out_swaps(chunk))
+            out_swap(chunk).start()
 
         @pl.when(stays)
         def _():
-            start(out_own(chunk))
+            out_own(chunk).start()
 
     transport(3, state3, last, done)
 
@@ -544,12 +530,22 @@
     def _():
         vel_swap.wait_send()
         for chunk in chunks:
-            for copy in swaps(0, chunk) + swaps(1, chunk) + swaps(2, chunk) + out_swaps(chunk):
+            for copy in [swap(level, chunk) for level in range(3)] + [out_swap(chunk)]:
                 copy.wait_send()
 
     for chunk in chunks:
-        for at, (src, dst) in enumerate(outs(chunk)):
-            pltpu.make_async_copy(dst, dst, o_recv.at[chunk, at]).wait()
+        out_own(chunk).wait()
+
+
+def hand_out(next_ref, conc_out, therm_out, sem):
+    copies = [
+        pltpu.make_async_copy(next_ref.at[0:SPECIES], conc_out, sem.at[0]),
+        pltpu.make_async_copy(next_ref.at[SPECIES], therm_out, sem.at[1]),
+    ]
+    for copy in copies:
+        copy.start()
+    for copy in copies:
+        copy.wait()
 
 
 def local(
@@ -570,7 +566,7 @@
     parts = len(CHUNKS)
     dma = pltpu.SemaphoreType.DMA
     scratch = [
-        pltpu.VMEM((2,) + block, f32),
+        pltpu.VMEM((3,) + block, f32),
         pltpu.VMEM(block, f32),
         pltpu.VMEM(block, f32),
         pltpu.VMEM(wide, f32),
@@ -588,8 +584,8 @@
         pltpu.VMEM(block, f32),
         pltpu.VMEM((2 * QROWS, LANES), bf16),
         pltpu.VMEM((FIELDS, CZ, LANES), f32),
-        pltpu.VMEM((CX, ROWS, 2 * CY), bf16),
-        pltpu.VMEM((CX, ROWS, 2 * CY), bf16),
+        pltpu.VMEM((CX * ROWS, 2 * CY), bf16),
+        pltpu.VMEM((CX * ROWS, 2 * CY), bf16),
         pltpu.VMEM((CX, FIELDS, CZ, 2 * CY), f32),
         pltpu.VMEM((FIELDS, CZ, LANES), f32),
         pltpu.VMEM((FIELDS, CZ, LANES), f32),
@@ -609,33 +605,31 @@
         pltpu.SMEM((1, SPECIES), f32),
         pltpu.SMEM((1, FIELDS), f32),
         pltpu.VMEM((4, REACT), jnp.int32),
+        pltpu.VMEM((3, CX, CZ, CY), f32),
         dma((parts, 2)),
-        dma((9,)),
+        dma((10,)),
         dma((2,)),
-        dma((3, parts, 2)),
-        dma((3, parts, 2)),
+        dma((3, parts)),
+        dma((3, parts)),
         dma((3, 2, parts)),
         dma((3, 2, parts)),
         dma((4, parts)),
         dma((4, parts)),
         dma((4,)),
         dma((4,)),
-        dma((parts, 2)),
-        dma((parts, 2)),
+        dma((parts,)),
+        dma((parts,)),
     ]
-    return pl.pallas_call(
+    stepped = pl.pallas_call(
         functools.partial(kernel, n_gx),
-        out_shape=(
-            jax.ShapeDtypeStruct((SPECIES, CX, CZ, CY), f32),
-            jax.ShapeDtypeStruct((CX, CZ, CY), f32),
-        ),
+        out_shape=pltpu.VMEM(block, f32),
         in_specs=[any_space] * 11,
-        out_specs=(any_space, any_space),
+        out_specs=any_space,
         scratch_shapes=scratch,
         compiler_params=pltpu.CompilerParams(
-            collective_id=0, has_side_effects=True, vmem_limit_bytes=64 * 1024 * 1024
+            collective_id=0, has_side_effects=True, vmem_limit_bytes=40 * 1024 * 1024
         ),
-    )(
+    )(*[pltpu.with_memory_space_constraint(value, pltpu.HBM) for value in (
         concentration_levels,
         thermal_levels,
         fluid_velocity,
@@ -647,7 +641,18 @@
         jnp.asarray(y_matrix()),
         jnp.asarray(edge_matrix()),
         jnp.asarray(z_matrix()),
-    )
+    )])
+    return pl.pallas_call(
+        hand_out,
+        out_shape=(
+            jax.ShapeDtypeStruct((SPECIES, CX, CZ, CY), f32),
+            jax.ShapeDtypeStruct((CX, CZ, CY), f32),
+        ),
+        in_specs=[any_space],
+        out_specs=(any_space, any_space),
+        scratch_shapes=[dma((2,))],
+        compiler_params=pltpu.CompilerParams(vmem_limit_bytes=8 * 1024 * 1024),
+    )(stepped)
 
 
 def solution(mesh):

time: 50.6 us -> 49.4 us (0.976)
  local copies, waits for them, and re-layouts: 2.3 us -> 0 us
  Pallas kernels: 47.5 us -> 48.6 us
    unnamed x4 -> x0, local copies, waits for them, and re-layouts: 2.3 us -> none
    pallas_call x1 -> x2, Pallas kernels: 47.5 us -> 48.6 us  [the longest x1 47.9 us: local(): pl.pallas_call(functools.partial(kernel, n_gx), out_shape=pltpu.VMEM(bloc...]
where the time goes in v2:
time: 49.4 us; the launch traced here: 49.2 us
  Pallas kernels  48.6 us (98%)
  between operations  0.64 us (1%)
    pallas_call x1, Pallas kernels, local(): pl.pallas_call(functools.partial(kernel, n_gx), out_shape=pltpu.VMEM(bloc...  47.9 us

profile of v2, /device:TPU:1, one launch (start us, length us, event | category | flops | bytes accessed | tf_op | source)
XLA Modules:
  0.0 49.2 jit_solution(1120171866272163496)
XLA Ops:
  0.6 47.9 %shard_map.122.next_ref = f32[18,4,8,128]{3,2,1,0:T(8,128)S(1)} custom-call(f32[3,17,4,8,128]{4,3,2,1,0:T(8,128)} %conc.1, f32[3,4,8,128]{3,2,1,0:T(8,128)} %therm.1, f32[3,4,8,128]{3,2,1,0:T(8,128)} %veloc.1, s32[4,73]{1,0:T(4,128)} %table_h.1, f32[1,73]{1,0:T(1,128)} %bitcast.4, f32[1,73]{1,0:T(1,128)} %bitcast.5, f32[1,17]{1,0:T(1,128)} %bitcast.6, ...), custom_call_target="tpu_custom_call" | custom-call | tf_op jit(solution)/shard_map/pallas_call | solution.py:623
  48.5 0.7 %shard_map.123 = (f32[17,4,8,128]{3,2,1,0:T(8,128)}, f32[4,8,128]{2,1,0:T(8,128)}) custom-call(f32[18,4,8,128]{3,2,1,0:T(8,128)S(1)} %shard_map.122.next_ref), custom_call_target="tpu_custom_call" | custom-call | tf_op jit(solution)/shard_map/pallas_call | solution.py:645

commit v3 on v2

--- a/solution.py
+++ b/solution.py
@@ -20,6 +20,7 @@
 QUADS = (FIELDS + QUAD - 1) // QUAD
 QROWS = 640
 CHUNKS = ((0, 8), (8, 16), (16, 18))
+BESIDE = (1,)
 
 time_step = 0.125
 first_coeffs = (4.0 / 5.0, -1.0 / 5.0, 4.0 / 105.0, -1.0 / 280.0)
@@ -102,7 +103,7 @@
     rate, local, result, qbuf, made, parts, near, dy, dz1, dz2, edge, kpack, vpack, nuk,
     ymat, emat, zmat, ymat_v, emat_v, zmat_v,
     table_s, logs, barriers, heats, kappas, table_v,
-    vel_near, past_sem, ld_sem, vel_send, swap_send, arrive, x_send, x_recv, z_send, z_recv, y_send, y_recv,
+    vel_near, relay, hop_send, hop_recv, on_send, past_sem, ld_sem, vel_send, swap_send, arrive, x_send, x_recv, z_send, z_recv, y_send, y_recv,
     o_send, o_recv,
 ):
     gx, gy, gz = lax.axis_index("gx"), lax.axis_index("gy"), lax.axis_index("gz")
@@ -165,6 +166,19 @@
         src, dst = moved(level, chunk)
         return remote(src, dst, swap_send.at[level, chunk], arrive.at[level, chunk], opposite)
 
+    def hop(chunk):
+        span = slice(*CHUNKS[chunk])
+        return remote(
+            past.at[2, span], relay.at[0, span], hop_send.at[chunk], hop_recv.at[0, chunk],
+            z_partner,
+        )
+
+    def on(chunk):
+        span = slice(*CHUNKS[chunk])
+        return remote(
+            relay.at[0, span], lev_c.at[span], on_send.at[0, chunk], arrive.at[2, chunk], y_partner
+        )
+
     def own(level, chunk):
         src, dst = moved(level, chunk)
         return pltpu.make_async_copy(src, dst, arrive.at[level, chunk])
@@ -222,11 +236,11 @@
     @pl.when(moves)
     def _():
         for chunk in chunks:
+            hop(chunk).start()
             swap(0, chunk).start()
         vel_swap.start()
-        for level in (2, 1):
-            for chunk in chunks:
-                swap(level, chunk).start()
+        for chunk in chunks:
+            swap(1, chunk).start()
 
     for load in loads[:-1]:
         load.wait()
@@ -433,6 +447,12 @@
     def keep(f, x, value):
         local[f, x] = value
 
+    @pl.when(stays)
+    def _():
+        for chunk in chunks:
+            hop(chunk).wait_recv()
+            on(chunk).start()
+
     for chunk in chunks:
         placed(2, chunk)
         send_borders(0, lev_c, chunk)
@@ -444,6 +464,12 @@
                 start(x_copies(level, chunk, past.at[level]))
 
     reactions(lev_c)
+
+    @pl.when(moves)
+    def _():
+        placed(1, 0)
+        start(x_copies(1, 0))
+
 
     vel_own.wait()
     for x in range(CX):
@@ -454,7 +480,7 @@
 
     @pl.when(moves)
     def _():
-        for chunk in chunks:
+        for chunk in chunks[1:]:
             placed(1, chunk)
             start(x_copies(1, chunk))
         for chunk in chunks:
@@ -500,7 +526,16 @@
 
     def out_swap(chunk):
         src, dst = outs(chunk)
-        return remote(src, dst, o_send.at[chunk], o_recv.at[chunk], opposite)
+        where, recv = opposite, o_recv.at[chunk]
+        if chunk in BESIDE:
+            dst, where, recv = relay.at[1, slice(*CHUNKS[chunk])], z_partner, hop_recv.at[1, chunk]
+        return remote(src, dst, o_send.at[chunk], recv, where)
+
+    def out_on(chunk):
+        span = slice(*CHUNKS[chunk])
+        return remote(
+            relay.at[1, span], next_out.at[span], on_send.at[1, chunk], o_recv.at[chunk], y_partner
+        )
 
     def out_own(chunk):
         src, dst = outs(chunk)
@@ -517,6 +552,12 @@
 
     transport(3, state3, last, done)
 
+    @pl.when(stays)
+    def _():
+        for chunk in BESIDE:
+            out_swap(chunk).wait_recv()
+            out_on(chunk).start()
+
     for level in range(3):
         for chunk in chunks:
             for copy in x_copies(level, chunk):
@@ -530,8 +571,15 @@
     def _():
         vel_swap.wait_send()
         for chunk in chunks:
-            for copy in [swap(level, chunk) for level in range(3)] + [out_swap(chunk)]:
+            for copy in (swap(0, chunk), swap(1, chunk), hop(chunk), out_swap(chunk)):
                 copy.wait_send()
+
+    @pl.when(stays)
+    def _():
+        for chunk in chunks:
+            on(chunk).wait_send()
+        for chunk in BESIDE:
+            out_on(chunk).wait_send()
 
     for chunk in chunks:
         out_own(chunk).wait()
@@ -606,6 +654,10 @@
         pltpu.SMEM((1, FIELDS), f32),
         pltpu.VMEM((4, REACT), jnp.int32),
         pltpu.VMEM((3, CX, CZ, CY), f32),
+        pltpu.VMEM((2,) + block, f32),
+        dma((parts,)),
+        dma((2, parts)),
+        dma((2, parts)),
         dma((parts, 2)),
         dma((10,)),
         dma((2,)),

time: 49.4 us -> 49.5 us (level)
  no operation moved by 1% of the time
where the time goes in v3:
time: 49.5 us; the launch traced here: 49.4 us
  Pallas kernels  48.7 us (98%)
  between operations  0.64 us (1%)
    pallas_call x1, Pallas kernels, local(): pl.pallas_call(functools.partial(kernel, n_gx), out_shape=pltpu.VMEM(bloc...  48 us

profile of v3, /device:TPU:1, one launch (start us, length us, event | category | flops | bytes accessed | tf_op | source)
XLA Modules:
  0.0 49.4 jit_solution(5707317611722379602)
XLA Ops:
  0.6 48.0 %shard_map.122.next_ref = f32[18,4,8,128]{3,2,1,0:T(8,128)S(1)} custom-call(f32[3,17,4,8,128]{4,3,2,1,0:T(8,128)} %conc.1, f32[3,4,8,128]{3,2,1,0:T(8,128)} %therm.1, f32[3,4,8,128]{3,2,1,0:T(8,128)} %veloc.1, s32[4,73]{1,0:T(4,128)} %table_h.1, f32[1,73]{1,0:T(1,128)} %bitcast.4, f32[1,73]{1,0:T(1,128)} %bitcast.5, f32[1,17]{1,0:T(1,128)} %bitcast.6, ...), custom_call_target="tpu_custom_call" | custom-call | tf_op jit(solution)/shard_map/pallas_call | solution.py:675
  48.6 0.7 %shard_map.123 = (f32[17,4,8,128]{3,2,1,0:T(8,128)}, f32[4,8,128]{2,1,0:T(8,128)}) custom-call(f32[18,4,8,128]{3,2,1,0:T(8,128)S(1)} %shard_map.122.next_ref), custom_call_target="tpu_custom_call" | custom-call | tf_op jit(solution)/shard_map/pallas_call | solution.py:697

commit v4 on v3

--- a/solution.py
+++ b/solution.py
@@ -20,7 +20,7 @@
 QUADS = (FIELDS + QUAD - 1) // QUAD
 QROWS = 640
 CHUNKS = ((0, 8), (8, 16), (16, 18))
-BESIDE = (1,)
+BESIDE = (0,)
 
 time_step = 0.125
 first_coeffs = (4.0 / 5.0, -1.0 / 5.0, 4.0 / 105.0, -1.0 / 280.0)
@@ -343,7 +343,7 @@
                 qbuf[pl.ds(QROWS + begin, 16), lanes] = low
             return carry
 
-        lax.fori_loop(0, (REACT + 1) // 2, two, 0, unroll=4)
+        lax.fori_loop(0, (REACT + 1) // 2, two, 0, unroll=8)
 
     def in_parts(source, into):
         for f in range(0, FIELDS, 2):

time: 49.5 us -> 49.7 us (level)
  no operation moved by 1% of the time
where the time goes in v4:
time: 49.7 us; the launch traced here: 49.6 us
  Pallas kernels  48.9 us (98%)
  between operations  0.64 us (1%)
    pallas_call x1, Pallas kernels, local(): pl.pallas_call(functools.partial(kernel, n_gx), out_shape=pltpu.VMEM(bloc...  48.2 us

profile of v4, /device:TPU:1, one launch (start us, length us, event | category | flops | bytes accessed | tf_op | source)
XLA Modules:
  0.0 49.6 jit_solution(8416471008831752778)
XLA Ops:
  0.6 48.2 %shard_map.122.next_ref = f32[18,4,8,128]{3,2,1,0:T(8,128)S(1)} custom-call(f32[3,17,4,8,128]{4,3,2,1,0:T(8,128)} %conc.1, f32[3,4,8,128]{3,2,1,0:T(8,128)} %therm.1, f32[3,4,8,128]{3,2,1,0:T(8,128)} %veloc.1, s32[4,73]{1,0:T(4,128)} %table_h.1, f32[1,73]{1,0:T(1,128)} %bitcast.4, f32[1,73]{1,0:T(1,128)} %bitcast.5, f32[1,17]{1,0:T(1,128)} %bitcast.6, ...), custom_call_target="tpu_custom_call" | custom-call | tf_op jit(solution)/shard_map/pallas_call | solution.py:675
  48.8 0.7 %shard_map.123 = (f32[17,4,8,128]{3,2,1,0:T(8,128)}, f32[4,8,128]{2,1,0:T(8,128)}) custom-call(f32[18,4,8,128]{3,2,1,0:T(8,128)S(1)} %shard_map.122.next_ref), custom_call_target="tpu_custom_call" | custom-call | tf_op jit(solution)/shard_map/pallas_call | solution.py:697

commit v5 on v3

--- a/solution.py
+++ b/solution.py
@@ -241,6 +241,12 @@
         vel_swap.start()
         for chunk in chunks:
             swap(1, chunk).start()
+
+    @pl.when(stays)
+    def _():
+        for chunk in chunks:
+            hop(chunk).wait_recv()
+            on(chunk).start()
 
     for load in loads[:-1]:
         load.wait()
@@ -446,12 +452,6 @@
 
     def keep(f, x, value):
         local[f, x] = value
-
-    @pl.when(stays)
-    def _():
-        for chunk in chunks:
-            hop(chunk).wait_recv()
-            on(chunk).start()
 
     for chunk in chunks:
         placed(2, chunk)

time: 49.5 us -> 49.5 us (level)
  no operation moved by 1% of the time
where the time goes in v5:
time: 49.5 us; the launch traced here: 49.4 us
  Pallas kernels  48.7 us (98%)
  between operations  0.64 us (1%)
    pallas_call x1, Pallas kernels, local(): pl.pallas_call(functools.partial(kernel, n_gx), out_shape=pltpu.VMEM(bloc...  48 us

profile of v5, /device:TPU:1, one launch (start us, length us, event | category | flops | bytes accessed | tf_op | source)
XLA Modules:
  0.0 49.4 jit_solution(8614628651028125349)
XLA Ops:
  0.6 48.0 %shard_map.122.next_ref = f32[18,4,8,128]{3,2,1,0:T(8,128)S(1)} custom-call(f32[3,17,4,8,128]{4,3,2,1,0:T(8,128)} %conc.1, f32[3,4,8,128]{3,2,1,0:T(8,128)} %therm.1, f32[3,4,8,128]{3,2,1,0:T(8,128)} %veloc.1, s32[4,73]{1,0:T(4,128)} %table_h.1, f32[1,73]{1,0:T(1,128)} %bitcast.4, f32[1,73]{1,0:T(1,128)} %bitcast.5, f32[1,17]{1,0:T(1,128)} %bitcast.6, ...), custom_call_target="tpu_custom_call" | custom-call | tf_op jit(solution)/shard_map/pallas_call | solution.py:675
  48.6 0.7 %shard_map.123 = (f32[17,4,8,128]{3,2,1,0:T(8,128)}, f32[4,8,128]{2,1,0:T(8,128)}) custom-call(f32[18,4,8,128]{3,2,1,0:T(8,128)S(1)} %shard_map.122.next_ref), custom_call_target="tpu_custom_call" | custom-call | tf_op jit(solution)/shard_map/pallas_call | solution.py:697
